TPU v7x, 256 devices: a whole 4x4x8 slice. The times are simulated.
256 devices in a mesh: px: 8 (over z), py: 32 (over x, y, core).
Axes of the slice: x: 4, y: 4, z: 8, core: 2. Of those that a mesh axis runs over, the one named last changes fastest.
Arguments:
- right_side: float32 [8, 2048, 2048], P(None, 'py', 'px'), may hold values from -6 to 6
- solution_in: float32 [8, 2048, 2048], P(None, 'py', 'px'), may hold values from -4 to 4
- classes: int32 [8, 2048, 2048], P(None, 'py', 'px'), may hold values from 0 to 15
- coeff_table: float32 [16], replicated, may hold values from 0.2 to 5
- eigenvectors: bfloat16 [2048, 2048], replicated, may hold values from -0.053880558 to 0.053880558, as said below
- eigenvalues: float32 [2048], replicated, may hold values from 0.01 to 4
- level_shift: float32 [8], replicated, may hold values from 0.3 to 3
Outputs:
- solution: float32 [8, 2048, 2048], P(None, 'py', 'px')
- residual: float32 [8, 2048, 2048], P(None, 'py', 'px')
- direction: float32 [8, 2048, 2048], P(None, 'py', 'px')
Inputs may be any that keep to these rules, and one draw needn't show every extreme that they name: eigenvectors is a symmetric matrix.
All inputs are finite; a program needn't handle non-finite values.
Results may differ from a plain program's by a relative error of at most 0.034.
Values may be sent and summed in bfloat16 or wider, within the bound.
A program may use at most 64 MiB of HBM per device.

v0:
```python
import jax
import jax.numpy as jnp
from jax import lax
from jax.sharding import PartitionSpec as P

ITERS = 2


def padded_2(array, sides, width):
    for axis, dim in sides:
        size, length = (lax.axis_size(axis), array.shape[dim])
        up = [(i, (i + 1) % size) for i in range(size - 1)]
        down = [(j, i) for i, j in up]
        last = lax.slice_in_dim(array, length - width, length, axis=dim)
        initial = lax.slice_in_dim(array, 0, width, axis=dim)
        before = lax.ppermute(last, axis, up)
        after = lax.ppermute(initial, axis, down)
        array = jnp.concatenate([before, array, after], axis=dim)
    return array


def for_sending(array):

    def short(part):
        return part.astype(jnp.bfloat16) if part.dtype == jnp.float32 else part

    return jax.tree.map(short, array)


def face_sum(padded, coeff_pad):
    values = padded[:, 1:-1, 1:-1]
    coeff = coeff_pad[:, 1:-1, 1:-1]
    height = values.shape[1]
    width = values.shape[2]
    result = jnp.zeros_like(values)
    for shift_y, shift_x in ((0, 1), (2, 1), (1, 0), (1, 2)):
        neighbour = padded[:, shift_y : shift_y + height, shift_x : shift_x + width]
        other = coeff_pad[:, shift_y : shift_y + height, shift_x : shift_x + width]
        result = result + 0.5 * (coeff + other) * (values - neighbour)
    vertical = 0.5 * (coeff[:-1] + coeff[1:]) * (values[:-1] - values[1:])
    zero_layer = jnp.zeros_like(values[:1])
    result = (
        result
        + jnp.concatenate((vertical, zero_layer), 0)
        - jnp.concatenate((zero_layer, vertical), 0)
    )
    return result


def precondition(residual, eigenvectors, eigenvalues, level_shift):
    rounded = residual.astype(jnp.bfloat16)
    levels_here = residual.shape[0] // lax.axis_size("px")
    first = jnp.einsum(
        "kyx,xi->kyi",
        lax.all_to_all(rounded, "px", split_axis=0, concat_axis=2, tiled=True),
        eigenvectors,
        preferred_element_type=jnp.float32,
    ).astype(jnp.bfloat16)
    second = jnp.einsum(
        "kyi,yj->kji",
        lax.all_to_all(first, "py", split_axis=2, concat_axis=1, tiled=True),
        eigenvectors,
        preferred_element_type=jnp.float32,
    )
    spectral_cols = second.shape[2]
    eigen_cols = lax.dynamic_slice_in_dim(
        eigenvalues, lax.axis_index("py") * spectral_cols, spectral_cols, 0
    )
    shift_here = lax.dynamic_slice_in_dim(
        level_shift, lax.axis_index("px") * levels_here, levels_here, 0
    )
    denom = eigenvalues[None, :, None] + eigen_cols[None, None, :] + shift_here[:, None, None]
    scaled = (second / denom).astype(jnp.bfloat16)
    fourth = jnp.einsum(
        "kji,yj->kyi", scaled, eigenvectors, preferred_element_type=jnp.float32
    ).astype(jnp.bfloat16)
    returned = lax.all_to_all(fourth, "py", split_axis=1, concat_axis=2, tiled=True)
    pencil = jnp.einsum("kyi,xi->kyx", returned, eigenvectors, preferred_element_type=jnp.float32)
    return lax.all_to_all(
        pencil.astype(jnp.bfloat16), "px", split_axis=2, concat_axis=0, tiled=True
    ).astype(pencil.dtype)


def shards(right_side, solution_in, classes, coeff_table, eigenvectors, eigenvalues, level_shift):
    coeff = jnp.zeros(classes.shape, jnp.float32)
    for label in range(coeff_table.shape[0]):
        coeff = jnp.where(classes == label, coeff_table[label], coeff)
    stacked = padded_2(
        jnp.stack((solution_in, coeff)).astype(jnp.bfloat16), (("px", 3), ("py", 2)), 1
    ).astype(jnp.float32)
    coeff_pad = stacked[1]
    solution = solution_in
    residual = right_side - face_sum(stacked[0], coeff_pad)
    direction = jnp.zeros_like(residual)
    gamma_prev = jnp.float32(1.0)
    for iteration in range(ITERS):
        precond = precondition(residual, eigenvectors, eigenvalues, level_shift)
        gamma = lax.psum(jnp.sum(residual * precond), ("px", "py"))
        if iteration == 0:
            direction = precond
        else:
            direction = precond + gamma / gamma_prev * direction
        padded = padded_2(for_sending(direction), (("px", 2), ("py", 1)), 1).astype(direction.dtype)
        image = face_sum(padded, coeff_pad)
        alpha = gamma / lax.psum(jnp.sum(direction * image), ("px", "py"))
        solution = solution + alpha * direction
        residual = residual - alpha * image
        gamma_prev = gamma
    return (solution, residual, direction)


def solution(mesh):
    in_specs = (P(None, "py", "px"), P(None, "py", "px"), P(None, "py", "px"), P(), P(), P(), P())
    out_specs = (P(None, "py", "px"), P(None, "py", "px"), P(None, "py", "px"))
    return jax.shard_map(shards, mesh=mesh, in_specs=in_specs, out_specs=out_specs, check_vma=False)
```

profile of v0, /device:TPU:1, one launch (start us, length us, event | category | flops | bytes accessed | tf_op | source)
XLA Modules:
  0.0 568.5 jit_solution(7523217841468684797)
XLA Ops:
  2.6 12.1 %fusion.53 = (bf16[1,8,64,256]{3,1,2,0:T(8,128)(2,1)S(1)}, bf16[1,8,64,256]{3,1,2,0:T(8,128)(2,1)S(1)}) fusion(f32[8,64,256]{2,1,0:T(8,128)} %param.8, bf16[]{:T(256)} %bitcast.16, bf16[]{:T(256)} %bitcast.15, bf16[]{:T(256)} %bitcast.14, bf16[]{:T(256)} %bitcast.13, bf16[]{:T(256)} %bitcast.12, bf16[]{:T(256)} %bitcast.11, bf16[]{:T(256)} %bitcast.10, ...), kind=kLoop, calls=%fused_computation.99 | loop fusion | flops 4194304 | bytes 1572896 | tf_op jit(solution)/shard_map/stack | solution.py:89
  40.9 18.6 %all_to_all.117 = bf16[8,64,256]{2,1,0:T(8,128)(2,1)S(1)} all-to-all(bf16[8,64,256]{2,1,0:T(8,128)(2,1)S(1)} %copy.132), channel_id=1, replica_groups=mesh['px'=8,'py'=32] {'px'}, dimensions={0} | all-to-all | bytes 524288 | tf_op jit(solution)/shard_map/all_to_all | solution.py:55
  62.5 11.5 %reduce = bf16[2048,64]{1,0:T(8,128)(2,1)S(1)} reduce(bf16[2048,1,64]{2,1,0:T(2,128)(2,1)S(1)} %bitcast.188, bf16[]{:T(256)} %broadcast.67), dimensions={1}, to_apply=%bitcast.140.reduce_sub_computation | reduce | bytes 524290
  75.1 9.1 %all-to-all-start.1 = ((bf16[32,2,2048]{2,1,0:T(2,128)(2,1)}), bf16[32,2,2048]{2,1,0:T(2,128)(2,1)S(1)}, u32[]{:S(2)}, u32[]{:S(2)}) async-start(bf16[32,2,2048]{2,1,0:T(2,128)(2,1)} %reshape.79), calls=%async_computation.1 | async-start | bytes 524288 | tf_op jit(solution)/shard_map/all_to_all | solution.py:61
  84.9 8.2 %all-to-all-done.1 = bf16[32,2,2048]{2,1,0:T(2,128)(2,1)S(1)} async-done(((bf16[32,2,2048]{2,1,0:T(2,128)(2,1)}), bf16[32,2,2048]{2,1,0:T(2,128)(2,1)S(1)}, u32[]{:S(2)}, u32[]{:S(2)}) %all-to-all-start.1) | async-done | bytes 262176 | tf_op jit(solution)/shard_map/all_to_all | solution.py:61
  96.5 10.6 %fusion.5 = bf16[1,2048,64]{1,2,0:T(8,128)(2,1)S(1)} fusion(bf16[2048,2048]{1,0:T(8,128)(2,1)} %param.11, bf16[2048,64]{0,1:T(8,128)(2,1)S(1)} %reshape.72, f32[]{:T(128)} %bitcast.25, f32[64]{0:T(128)S(1)} %dynamic_slice.8, f32[2048]{0:T(1024)S(1)} %copy-done.2), kind=kOutput, calls=%fused_computation.13 | convolution fusion | flops 1074397184 | bytes 8921348 | tf_op jit(solution)/shard_map/kji,yj->kyi/dot_general | solution.py:74
  107.8 11.5 %reduce.1 = bf16[2048,64]{1,0:T(8,128)(2,1)S(1)} reduce(bf16[2048,1,64]{2,1,0:T(2,128)(2,1)S(1)} %bitcast.190, bf16[]{:T(256)} %broadcast.67), dimensions={1}, to_apply=%bitcast.142.reduce_sub_computation | reduce | bytes 524290
  119.7 12.6 %all_to_all.118 = bf16[32,2,2048]{2,1,0:T(2,128)(2,1)S(1)} all-to-all(bf16[32,2,2048]{2,1,0:T(2,128)(2,1)S(1)} %reshape.81), channel_id=1, replica_groups=mesh['px'=8,'py'=32] {'py'}, dimensions={0} | all-to-all | bytes 524288 | tf_op jit(solution)/shard_map/all_to_all | solution.py:77
  135.6 6.0 %fusion.6 = bf16[1,64,2048]{2,1,0:T(8,128)(2,1)S(1)} fusion(bf16[64,2048]{1,0:T(8,128)(2,1)S(1)} %reshape.73, bf16[2048,2048]{1,0:T(8,128)(2,1)} %param.11), kind=kOutput, calls=%fused_computation.14 | convolution fusion | flops 537001984 | bytes 8912896 | tf_op jit(solution)/shard_map/kyi,xi->kyx/dot_general | solution.py:78
  142.4 11.5 %reduce.2 = bf16[2048,64]{1,0:T(8,128)(2,1)S(1)} reduce(bf16[2048,1,64]{2,1,0:T(2,128)(2,1)S(1)} %bitcast.191, bf16[]{:T(256)} %broadcast.67), dimensions={1}, to_apply=%bitcast.144.reduce_sub_computation | reduce | bytes 524290
  154.4 14.8 %all_to_all.119 = bf16[8,2,8192]{2,1,0:T(2,128)(2,1)S(1)} all-to-all(bf16[8,2,8192]{2,1,0:T(2,128)(2,1)S(1)} %reshape.83), channel_id=1, replica_groups=mesh['px'=8,'py'=32] {'px'}, dimensions={0} | all-to-all | bytes 524288 | tf_op jit(solution)/shard_map/all_to_all | solution.py:79
  190.1 75.7 %all-reduce.6 = (f32[]{:T(128)}, f32[]{:T(128)}) all-reduce(f32[]{:T(128)} %get-tuple-element.13, f32[]{:T(128)} %get-tuple-element.12), channel_id=1, replica_groups=mesh['px'=8,'py'=32] {'px','py'}, use_global_device_ids=true, to_apply=%region_1.2 | all-reduce | flops 2 | bytes 16 | tf_op jit(solution)/shard_map/psum | solution.py:98
  267.2 14.4 %all_to_all.120 = bf16[8,64,256]{2,1,0:T(8,128)(2,1)S(1)} all-to-all(bf16[8,64,256]{2,1,0:T(8,128)(2,1)S(1)} %copy.143), channel_id=1, replica_groups=mesh['px'=8,'py'=32] {'px'}, dimensions={0} | all-to-all | bytes 524288 | tf_op jit(solution)/shard_map/all_to_all | solution.py:55
  281.7 5.0 fusion.7
  287.4 11.5 %reduce.3 = bf16[2048,64]{1,0:T(8,128)(2,1)S(1)} reduce(bf16[2048,1,64]{2,1,0:T(2,128)(2,1)S(1)} %bitcast.192, bf16[]{:T(256)} %broadcast.67), dimensions={1}, to_apply=%bitcast.146.reduce_sub_computation | reduce | bytes 524290
  299.4 15.9 %all_to_all.121 = bf16[32,2,2048]{2,1,0:T(2,128)(2,1)S(1)} all-to-all(bf16[32,2,2048]{2,1,0:T(2,128)(2,1)S(1)} %reshape.85), channel_id=1, replica_groups=mesh['px'=8,'py'=32] {'py'}, dimensions={0} | all-to-all | bytes 524288 | tf_op jit(solution)/shard_map/all_to_all | solution.py:61
  318.6 10.6 %fusion.8 = bf16[1,2048,64]{1,2,0:T(8,128)(2,1)S(1)} fusion(bf16[2048,2048]{1,0:T(8,128)(2,1)} %param.11, bf16[2048,64]{0,1:T(8,128)(2,1)S(1)} %reshape.75, f32[]{:T(128)} %bitcast.25, f32[64]{0:T(128)S(1)} %dynamic_slice.8, f32[2048]{0:T(1024)S(1)} %copy-done.2), kind=kOutput, calls=%fused_computation.16 | convolution fusion | flops 1074397184 | bytes 8921348 | tf_op jit(solution)/shard_map/kji,yj->kyi/dot_general | solution.py:74
  329.9 11.5 %reduce.4 = bf16[2048,64]{1,0:T(8,128)(2,1)S(1)} reduce(bf16[2048,1,64]{2,1,0:T(2,128)(2,1)S(1)} %bitcast.193, bf16[]{:T(256)} %broadcast.67), dimensions={1}, to_apply=%bitcast.148.reduce_sub_computation | reduce | bytes 524290
  341.8 12.6 %all_to_all.122 = bf16[32,2,2048]{2,1,0:T(2,128)(2,1)S(1)} all-to-all(bf16[32,2,2048]{2,1,0:T(2,128)(2,1)S(1)} %reshape.87), channel_id=1, replica_groups=mesh['px'=8,'py'=32] {'py'}, dimensions={0} | all-to-all | bytes 524288 | tf_op jit(solution)/shard_map/all_to_all | solution.py:77
  357.8 6.0 %fusion.9 = bf16[1,64,2048]{2,1,0:T(8,128)(2,1)S(1)} fusion(bf16[64,2048]{1,0:T(8,128)(2,1)S(1)} %reshape.76, bf16[2048,2048]{1,0:T(8,128)(2,1)} %param.11), kind=kOutput, calls=%fused_computation.17 | convolution fusion | flops 537001984 | bytes 8912896 | tf_op jit(solution)/shard_map/kyi,xi->kyx/dot_general | solution.py:78
  364.6 11.5 %reduce.5 = bf16[2048,64]{1,0:T(8,128)(2,1)S(1)} reduce(bf16[2048,1,64]{2,1,0:T(2,128)(2,1)S(1)} %bitcast.189, bf16[]{:T(256)} %broadcast.67), dimensions={1}, to_apply=%bitcast.150.reduce_sub_computation | reduce | bytes 524290
  376.5 14.8 %all_to_all.123 = bf16[8,2,8192]{2,1,0:T(2,128)(2,1)S(1)} all-to-all(bf16[8,2,8192]{2,1,0:T(2,128)(2,1)S(1)} %reshape.89), channel_id=1, replica_groups=mesh['px'=8,'py'=32] {'px'}, dimensions={0} | all-to-all | bytes 524288 | tf_op jit(solution)/shard_map/all_to_all | solution.py:79
  393.3 73.0 %psum.30 = f32[]{:T(128)} all-reduce(f32[]{:T(128)} %fusion.16), channel_id=1, replica_groups=mesh['px'=8,'py'=32] {'px','py'}, use_global_device_ids=true, to_apply=%region_5.6 | all-reduce | flops 1 | bytes 8 | tf_op jit(solution)/shard_map/psum | solution.py:98
  488.8 75.8 %psum.31 = f32[]{:T(128)} all-reduce(f32[]{:T(128)} %get-tuple-element.16), channel_id=1, replica_groups=mesh['px'=8,'py'=32] {'px','py'}, use_global_device_ids=true, to_apply=%region_7.8 | all-reduce | flops 1 | bytes 8 | tf_op jit(solution)/shard_map/psum | solution.py:105
  (109 shorter events, 98.2 us)
Async XLA Ops:
  0.6 39.0 %copy-start.1 = (f32[8,64,256]{2,1,0:T(8,128)S(1)}, f32[8,64,256]{2,1,0:T(8,128)}, u32[]{:S(2)}) copy-start(f32[8,64,256]{2,1,0:T(8,128)} %param.7) | copy-start | bytes 1572868
  14.8 9.3 %collective-permute-start = (bf16[2,8,64,1]{3,1,2,0:T(8,128)(2,1)S(1)}, bf16[2,8,64,1]{3,1,2,0:T(8,128)(2,1)S(1)}, u32[]{:S(2)}, u32[]{:S(2)}) collective-permute-start(bf16[2,8,64,1]{3,1,2,0:T(8,128)(2,1)S(1)} %get-tuple-element.33), channel_id=1, source_target_pairs={{0,32},{32,64},{64,96},{96,128},{128,160},{160,192},{192,224},{1,3... | collective-permute-start | bytes 6152 | tf_op jit(solution)/shard_map/ppermute | solution.py:16
  19.2 9.1 %collective-permute-start.1 = (bf16[2,8,64,1]{3,1,2,0:T(8,128)(2,1)S(1)}, bf16[2,8,64,1]{3,1,2,0:T(8,128)(2,1)S(1)}, u32[]{:S(2)}, u32[]{:S(2)}) collective-permute-start(bf16[2,8,64,1]{3,1,2,0:T(8,128)(2,1)S(1)} %get-tuple-element.34), channel_id=1, source_target_pairs={{32,0},{64,32},{96,64},{128,96},{160,128},{192,160},{224,192},{33,... | collective-permute-start | bytes 6152 | tf_op jit(solution)/shard_map/ppermute | solution.py:17
  28.4 7.0 %collective-permute-start.2 = (bf16[2,8,1,258]{3,1,2,0:T(8,128)(2,1)S(1)}, bf16[2,8,1,258]{3,1,2,0:T(8,128)(2,1)S(1)}, u32[]{:S(2)}, u32[]{:S(2)}) collective-permute-start(bf16[2,8,1,258]{3,1,2,0:T(8,128)(2,1)S(1)} %get-tuple-element.27), channel_id=1, source_target_pairs={{0,1},{1,2},{2,3},{3,4},{4,5},{5,6},{6,7},{7,8},{8,9},{9,10},{10,1... | collective-permute-start | bytes 24776 | tf_op jit(solution)/shard_map/ppermute | solution.py:16
  33.2 26.4 %slice-start = ((s8[8388608]{0:T(1024)(128)(4,1)}), s8[4194304]{0:T(1024)(128)(4,1)S(1)}, s32[]{:S(2)}) async-start(s8[8388608]{0:T(1024)(128)(4,1)} %bitcast.174), calls=%async_computation.8 | async-start | bytes 8388608
  33.2 5.3 collective-permute-start.3
  39.7 19.9 %slice-start.1 = ((s8[8388608]{0:T(1024)(128)(4,1)}), s8[4194304]{0:T(1024)(128)(4,1)S(1)}, s32[]{:S(2)}) async-start(s8[8388608]{0:T(1024)(128)(4,1)} %bitcast.174), calls=%async_computation.9 | async-start | bytes 8388608
  59.6 24.7 %copy-start.2 = (f32[2048]{0:T(1024)S(1)}, f32[2048]{0:T(1024)}, u32[]{:S(2)}) copy-start(f32[2048]{0:T(1024)} %param.12) | copy-start | bytes 24580
  59.6 24.7 %copy-start.3 = (f32[8]{0:T(128)S(1)}, f32[8]{0:T(128)}, u32[]{:S(2)}) copy-start(f32[8]{0:T(128)} %param.13) | copy-start | bytes 100
  75.1 18.0 %all-to-all-start.1 = ((bf16[32,2,2048]{2,1,0:T(2,128)(2,1)}), bf16[32,2,2048]{2,1,0:T(2,128)(2,1)S(1)}, u32[]{:S(2)}, u32[]{:S(2)}) async-start(bf16[32,2,2048]{2,1,0:T(2,128)(2,1)} %reshape.79), calls=%async_computation.1 | async-start | bytes 524288 | tf_op jit(solution)/shard_map/all_to_all | solution.py:61
  170.6 3.2 collective-permute-start.4
  171.9 5.7 %collective-permute-start.5 = (bf16[8,64,1]{2,0,1:T(8,128)(2,1)S(1)}, bf16[8,64,1]{2,0,1:T(8,128)(2,1)S(1)}, u32[]{:S(2)}, u32[]{:S(2)}) collective-permute-start(bf16[8,64,1]{2,0,1:T(8,128)(2,1)S(1)} %get-tuple-element.38), channel_id=1, source_target_pairs={{32,0},{64,32},{96,64},{128,96},{160,128},{192,160},{224,192},{33,... | collective-permute-start | bytes 3080 | tf_op jit(solution)/shard_map/ppermute | solution.py:17
  177.7 6.9 %collective-permute-start.6 = (bf16[8,1,258]{2,0,1:T(8,128)(2,1)S(1)}, bf16[8,1,258]{2,0,1:T(8,128)(2,1)S(1)}, u32[]{:S(2)}, u32[]{:S(2)}) collective-permute-start(bf16[8,1,258]{2,0,1:T(8,128)(2,1)S(1)} %get-tuple-element.31), channel_id=1, source_target_pairs={{0,1},{1,2},{2,3},{3,4},{4,5},{5,6},{6,7},{7,8},{8,9},{9,10},{10,1... | collective-permute-start | bytes 12392 | tf_op jit(solution)/shard_map/ppermute | solution.py:16
  182.5 4.9 collective-permute-start.7
  467.5 99.5 %copy-start = (f32[8,64,256]{2,1,0:T(8,128)S(1)}, f32[8,64,256]{2,1,0:T(8,128)}, u32[]{:S(2)}) copy-start(f32[8,64,256]{2,1,0:T(8,128)} %param.8) | copy-start | bytes 1572868
  467.7 5.9 %collective-permute-start.8 = (bf16[8,64,1]{2,0,1:T(8,128)(2,1)S(1)}, bf16[8,64,1]{2,0,1:T(8,128)(2,1)S(1)}, u32[]{:S(2)}, u32[]{:S(2)}) collective-permute-start(bf16[8,64,1]{2,0,1:T(8,128)(2,1)S(1)} %get-tuple-element.35), channel_id=1, source_target_pairs={{0,32},{32,64},{64,96},{96,128},{128,160},{160,192},{192,224},{1,3... | collective-permute-start | bytes 3080 | tf_op jit(solution)/shard_map/ppermute | solution.py:16
  471.4 5.7 %collective-permute-start.9 = (bf16[8,64,1]{2,0,1:T(8,128)(2,1)S(1)}, bf16[8,64,1]{2,0,1:T(8,128)(2,1)S(1)}, u32[]{:S(2)}, u32[]{:S(2)}) collective-permute-start(bf16[8,64,1]{2,0,1:T(8,128)(2,1)S(1)} %get-tuple-element.36), channel_id=1, source_target_pairs={{32,0},{64,32},{96,64},{128,96},{160,128},{192,160},{224,192},{33,... | collective-permute-start | bytes 3080 | tf_op jit(solution)/shard_map/ppermute | solution.py:17
  477.2 7.1 %collective-permute-start.10 = (bf16[8,1,258]{2,0,1:T(8,128)(2,1)S(1)}, bf16[8,1,258]{2,0,1:T(8,128)(2,1)S(1)}, u32[]{:S(2)}, u32[]{:S(2)}) collective-permute-start(bf16[8,1,258]{2,0,1:T(8,128)(2,1)S(1)} %get-tuple-element.29), channel_id=1, source_target_pairs={{0,1},{1,2},{2,3},{3,4},{4,5},{5,6},{6,7},{7,8},{8,9},{9,10},{10,1... | collective-permute-start | bytes 12392 | tf_op jit(solution)/shard_map/ppermute | solution.py:16
  481.2 4.9 collective-permute-start.11
where the time goes:
time: 578 us; the launch traced here: 569 us
  blocking collectives  328 us (57%)
  other arithmetic  90.5 us (16%)
  starting transfers between devices  42.4 us (7%)
  matrix products  39.8 us (7%)
  waiting for transfers between devices  32.6 us (6%)
  local copies, waits for them, and re-layouts  29.7 us (5%)
    psum x2, blocking collectives, shards(): gamma = lax.psum(jnp.sum(residual * precond), ('px', 'py'))  149 us
    psum x1, blocking collectives, shards(): alpha = gamma / lax.psum(jnp.sum(direction * image), ('px', 'py'))  75.8 us
    unnamed x7, other arithmetic  69.2 us
    all_to_all x2, blocking collectives, precondition(): lax.all_to_all(rounded, 'px', split_axis=0, concat_axis=2, tiled=True)  33 us
    all_to_all x2, blocking collectives, precondition(): lax.all_to_all(pencil.astype(jnp.bfloat16), 'px', split_axis=2, concat_ax...  29.6 us
    all_to_all x2, blocking collectives, precondition(): lax.all_to_all(fourth, 'py', split_axis=1, concat_axis=2, tiled=True)  25.3 us
    ppermute x6, starting transfers between devices, padded_2(): before = lax.ppermute(last, axis, up)  22.9 us
    dot_general x2, matrix products, precondition(): jnp.einsum('kji,yj->kyi', scaled, eigenvectors, preferred_element_type=jn...  21.1 us
  transfers between devices with their start and end apart: 13, of which 10 were waited for; matrix products, arithmetic and copies ran while one was open for 0% of the time, Pallas kernels for 0%

commit v1 on v0

--- a/solution.py
+++ b/solution.py
@@ -58,7 +58,10 @@
     ).astype(jnp.bfloat16)
     second = jnp.einsum(
         "kyi,yj->kji",
-        lax.all_to_all(first, "py", split_axis=2, concat_axis=1, tiled=True),
+        jnp.concatenate(
+            lax.all_to_all(jnp.stack(jnp.split(first, lax.axis_size("py"), axis=2)), "py", 0, 0),
+            axis=1,
+        ),
         eigenvectors,
         preferred_element_type=jnp.float32,
     )

time: 578 us -> 548 us (0.948)
  other arithmetic: 90.5 us -> 67.3 us
    unnamed x7 -> x5, other arithmetic: 69.2 us -> 46.2 us
    unnamed x32 -> x94, local copies, waits for them, and re-layouts: 10.3 us -> 12.8 us
where the time goes in v1:
time: 548 us; the launch traced here: 541 us
  blocking collectives  328 us (60%)
  other arithmetic  67.3 us (12%)
  starting transfers between devices  42.1 us (8%)
  matrix products  39.8 us (7%)
  waiting for transfers between devices  32.6 us (6%)
  local copies, waits for them, and re-layouts  25.6 us (5%)
  between operations  5.67 us (1%)
    psum x2, blocking collectives, shards(): gamma = lax.psum(jnp.sum(residual * precond), ('px', 'py'))  149 us
    psum x1, blocking collectives, shards(): alpha = gamma / lax.psum(jnp.sum(direction * image), ('px', 'py'))  75.8 us
    unnamed x5, other arithmetic  46.2 us
    all_to_all x2, blocking collectives, precondition(): lax.all_to_all(rounded, 'px', split_axis=0, concat_axis=2, tiled=True)  33 us
    all_to_all x2, blocking collectives, precondition(): lax.all_to_all(pencil.astype(jnp.bfloat16), 'px', split_axis=2, concat_ax...  29.6 us
    all_to_all x2, blocking collectives, precondition(): lax.all_to_all(fourth, 'py', split_axis=1, concat_axis=2, tiled=True)  25.5 us
    ppermute x6, starting transfers between devices, padded_2(): before = lax.ppermute(last, axis, up)  22.9 us
    dot_general x2, matrix products, precondition(): jnp.einsum('kji,yj->kyi', scaled, eigenvectors, preferred_element_type=jn...  21.2 us
  transfers between devices with their start and end apart: 13, of which 10 were waited for; matrix products, arithmetic and copies ran while one was open for 0% of the time, Pallas kernels for 0%

profile of v1, /device:TPU:1, one launch (start us, length us, event | category | flops | bytes accessed | tf_op | source)
XLA Modules:
  0.0 541.2 jit_solution(2820518403976896058)
XLA Ops:
  2.6 12.0 %fusion.53 = (bf16[1,8,64,256]{3,1,2,0:T(8,128)(2,1)S(1)}, bf16[1,8,64,256]{3,1,2,0:T(8,128)(2,1)S(1)}) fusion(f32[8,64,256]{2,1,0:T(8,128)} %param.8, bf16[]{:T(256)} %bitcast.16, bf16[]{:T(256)} %bitcast.15, bf16[]{:T(256)} %bitcast.14, bf16[]{:T(256)} %bitcast.13, bf16[]{:T(256)} %bitcast.12, bf16[]{:T(256)} %bitcast.11, bf16[]{:T(256)} %bitcast.10, ...), kind=kLoop, calls=%fused_computation.99 | loop fusion | flops 4194304 | bytes 1572896 | tf_op jit(solution)/shard_map/stack | solution.py:92
  28.4 4.8 collective-permute-start.2
  40.9 18.6 %all_to_all.97 = bf16[8,64,256]{2,1,0:T(8,128)(2,1)S(1)} all-to-all(bf16[8,64,256]{2,1,0:T(8,128)(2,1)S(1)} %copy.114), channel_id=1, replica_groups=mesh['px'=8,'py'=32] {'px'}, dimensions={0} | all-to-all | bytes 524288 | tf_op jit(solution)/shard_map/all_to_all | solution.py:55
  64.0 8.9 %all-to-all-start.1 = ((bf16[32,2,2048]{2,1,0:T(2,128)(2,1)}), bf16[32,2,2048]{2,1,0:T(2,128)(2,1)S(1)}, u32[]{:S(2)}, u32[]{:S(2)}) async-start(bf16[32,2,2048]{2,1,0:T(2,128)(2,1)} %reshape.81), calls=%async_computation.1 | async-start | bytes 524288 | tf_op jit(solution)/shard_map/all_to_all | solution.py:62
  73.5 8.2 %all-to-all-done.1 = bf16[32,2,2048]{2,1,0:T(2,128)(2,1)S(1)} async-done(((bf16[32,2,2048]{2,1,0:T(2,128)(2,1)}), bf16[32,2,2048]{2,1,0:T(2,128)(2,1)S(1)}, u32[]{:S(2)}, u32[]{:S(2)}) %all-to-all-start.1) | async-done | bytes 262176 | tf_op jit(solution)/shard_map/all_to_all | solution.py:62
  82.1 10.6 %fusion.5 = bf16[1,2048,64]{1,2,0:T(8,128)(2,1)S(1)} fusion(bf16[2048,2048]{1,0:T(8,128)(2,1)} %param.11, bf16[2048,64]{1,0:T(8,128)(2,1)S(1)} %bitcast.437, f32[]{:T(128)} %bitcast.57, f32[64]{0:T(128)S(1)} %dynamic_slice.8, f32[2048]{0:T(1024)S(1)} %copy-done.2), kind=kOutput, calls=%fused_computation.13 | convolution fusion | flops 1074397184 | bytes 8921348 | tf_op jit(solution)/shard_map/kji,yj->kyi/dot_general | solution.py:77
  93.9 11.5 %reduce = bf16[2048,64]{1,0:T(8,128)(2,1)S(1)} reduce(bf16[2048,1,64]{2,1,0:T(2,128)(2,1)S(1)} %bitcast.430, bf16[]{:T(256)} %broadcast.67), dimensions={1}, to_apply=%bitcast.388.reduce_sub_computation | reduce | bytes 524290
  105.9 12.9 %all_to_all.98 = bf16[32,2,2048]{2,1,0:T(2,128)(2,1)S(1)} all-to-all(bf16[32,2,2048]{2,1,0:T(2,128)(2,1)S(1)} %reshape.83), channel_id=1, replica_groups=mesh['px'=8,'py'=32] {'py'}, dimensions={0} | all-to-all | bytes 524288 | tf_op jit(solution)/shard_map/all_to_all | solution.py:80
  122.1 6.0 %fusion.6 = bf16[1,64,2048]{2,1,0:T(8,128)(2,1)S(1)} fusion(bf16[64,2048]{1,0:T(8,128)(2,1)S(1)} %reshape.75, bf16[2048,2048]{1,0:T(8,128)(2,1)} %param.11), kind=kOutput, calls=%fused_computation.14 | convolution fusion | flops 537001984 | bytes 8912896 | tf_op jit(solution)/shard_map/kyi,xi->kyx/dot_general | solution.py:81
  128.8 11.5 %reduce.1 = bf16[2048,64]{1,0:T(8,128)(2,1)S(1)} reduce(bf16[2048,1,64]{2,1,0:T(2,128)(2,1)S(1)} %bitcast.432, bf16[]{:T(256)} %broadcast.67), dimensions={1}, to_apply=%bitcast.390.reduce_sub_computation | reduce | bytes 524290
  140.8 14.8 %all_to_all.99 = bf16[8,2,8192]{2,1,0:T(2,128)(2,1)S(1)} all-to-all(bf16[8,2,8192]{2,1,0:T(2,128)(2,1)S(1)} %reshape.85), channel_id=1, replica_groups=mesh['px'=8,'py'=32] {'px'}, dimensions={0} | all-to-all | bytes 524288 | tf_op jit(solution)/shard_map/all_to_all | solution.py:82
  164.1 4.8 collective-permute-start.6
  176.5 75.7 %all-reduce.6 = (f32[]{:T(128)}, f32[]{:T(128)}) all-reduce(f32[]{:T(128)} %get-tuple-element.13, f32[]{:T(128)} %get-tuple-element.12), channel_id=1, replica_groups=mesh['px'=8,'py'=32] {'px','py'}, use_global_device_ids=true, to_apply=%region_1.2 | all-reduce | flops 2 | bytes 16 | tf_op jit(solution)/shard_map/psum | solution.py:101
  253.6 14.4 %all_to_all.100 = bf16[8,64,256]{2,1,0:T(8,128)(2,1)S(1)} all-to-all(bf16[8,64,256]{2,1,0:T(8,128)(2,1)S(1)} %copy.122), channel_id=1, replica_groups=mesh['px'=8,'py'=32] {'px'}, dimensions={0} | all-to-all | bytes 524288 | tf_op jit(solution)/shard_map/all_to_all | solution.py:55
  268.0 5.0 fusion.7
  275.1 15.5 %all_to_all.101 = bf16[32,2,2048]{2,1,0:T(2,128)(2,1)S(1)} all-to-all(bf16[32,2,2048]{2,1,0:T(2,128)(2,1)S(1)} %reshape.87), channel_id=1, replica_groups=mesh['px'=8,'py'=32] {'py'}, dimensions={0} | all-to-all | bytes 524288 | tf_op jit(solution)/shard_map/all_to_all | solution.py:62
  291.0 10.6 %fusion.8 = bf16[1,2048,64]{1,2,0:T(8,128)(2,1)S(1)} fusion(bf16[2048,2048]{1,0:T(8,128)(2,1)} %param.11, bf16[2048,64]{1,0:T(8,128)(2,1)S(1)} %bitcast.436, f32[]{:T(128)} %bitcast.57, f32[64]{0:T(128)S(1)} %dynamic_slice.8, f32[2048]{0:T(1024)S(1)} %copy-done.2), kind=kOutput, calls=%fused_computation.16 | convolution fusion | flops 1074397184 | bytes 8921348 | tf_op jit(solution)/shard_map/kji,yj->kyi/dot_general | solution.py:77
  302.3 11.5 %reduce.2 = bf16[2048,64]{1,0:T(8,128)(2,1)S(1)} reduce(bf16[2048,1,64]{2,1,0:T(2,128)(2,1)S(1)} %bitcast.433, bf16[]{:T(256)} %broadcast.67), dimensions={1}, to_apply=%bitcast.392.reduce_sub_computation | reduce | bytes 524290
  314.2 12.7 %all_to_all.102 = bf16[32,2,2048]{2,1,0:T(2,128)(2,1)S(1)} all-to-all(bf16[32,2,2048]{2,1,0:T(2,128)(2,1)S(1)} %reshape.89), channel_id=1, replica_groups=mesh['px'=8,'py'=32] {'py'}, dimensions={0} | all-to-all | bytes 524288 | tf_op jit(solution)/shard_map/all_to_all | solution.py:80
  330.2 6.0 %fusion.9 = bf16[1,64,2048]{2,1,0:T(8,128)(2,1)S(1)} fusion(bf16[64,2048]{1,0:T(8,128)(2,1)S(1)} %reshape.78, bf16[2048,2048]{1,0:T(8,128)(2,1)} %param.11), kind=kOutput, calls=%fused_computation.17 | convolution fusion | flops 537001984 | bytes 8912896 | tf_op jit(solution)/shard_map/kyi,xi->kyx/dot_general | solution.py:81
  337.0 11.5 %reduce.3 = bf16[2048,64]{1,0:T(8,128)(2,1)S(1)} reduce(bf16[2048,1,64]{2,1,0:T(2,128)(2,1)S(1)} %bitcast.431, bf16[]{:T(256)} %broadcast.67), dimensions={1}, to_apply=%bitcast.394.reduce_sub_computation | reduce | bytes 524290
  349.0 14.8 %all_to_all.103 = bf16[8,2,8192]{2,1,0:T(2,128)(2,1)S(1)} all-to-all(bf16[8,2,8192]{2,1,0:T(2,128)(2,1)S(1)} %reshape.91), channel_id=1, replica_groups=mesh['px'=8,'py'=32] {'px'}, dimensions={0} | all-to-all | bytes 524288 | tf_op jit(solution)/shard_map/all_to_all | solution.py:82
  365.8 73.0 %psum.30 = f32[]{:T(128)} all-reduce(f32[]{:T(128)} %fusion.16), channel_id=1, replica_groups=mesh['px'=8,'py'=32] {'px','py'}, use_global_device_ids=true, to_apply=%region_5.6 | all-reduce | flops 1 | bytes 8 | tf_op jit(solution)/shard_map/psum | solution.py:101
  461.3 75.8 %psum.31 = f32[]{:T(128)} all-reduce(f32[]{:T(128)} %get-tuple-element.16), channel_id=1, replica_groups=mesh['px'=8,'py'=32] {'px','py'}, use_global_device_ids=true, to_apply=%region_7.8 | all-reduce | flops 1 | bytes 8 | tf_op jit(solution)/shard_map/psum | solution.py:108
  (161 shorter events, 84.4 us)
Async XLA Ops:
  0.6 39.0 %copy-start.1 = (f32[8,64,256]{2,1,0:T(8,128)S(1)}, f32[8,64,256]{2,1,0:T(8,128)}, u32[]{:S(2)}) copy-start(f32[8,64,256]{2,1,0:T(8,128)} %param.7) | copy-start | bytes 1572868
  14.8 9.3 %collective-permute-start = (bf16[2,8,64,1]{3,1,2,0:T(8,128)(2,1)S(1)}, bf16[2,8,64,1]{3,1,2,0:T(8,128)(2,1)S(1)}, u32[]{:S(2)}, u32[]{:S(2)}) collective-permute-start(bf16[2,8,64,1]{3,1,2,0:T(8,128)(2,1)S(1)} %get-tuple-element.33), channel_id=1, source_target_pairs={{0,32},{32,64},{64,96},{96,128},{128,160},{160,192},{192,224},{1,3... | collective-permute-start | bytes 6152 | tf_op jit(solution)/shard_map/ppermute | solution.py:16
  19.2 9.1 %collective-permute-start.1 = (bf16[2,8,64,1]{3,1,2,0:T(8,128)(2,1)S(1)}, bf16[2,8,64,1]{3,1,2,0:T(8,128)(2,1)S(1)}, u32[]{:S(2)}, u32[]{:S(2)}) collective-permute-start(bf16[2,8,64,1]{3,1,2,0:T(8,128)(2,1)S(1)} %get-tuple-element.34), channel_id=1, source_target_pairs={{32,0},{64,32},{96,64},{128,96},{160,128},{192,160},{224,192},{33,... | collective-permute-start | bytes 6152 | tf_op jit(solution)/shard_map/ppermute | solution.py:17
  28.4 7.0 %collective-permute-start.2 = (bf16[2,8,1,258]{3,1,2,0:T(8,128)(2,1)S(1)}, bf16[2,8,1,258]{3,1,2,0:T(8,128)(2,1)S(1)}, u32[]{:S(2)}, u32[]{:S(2)}) collective-permute-start(bf16[2,8,1,258]{3,1,2,0:T(8,128)(2,1)S(1)} %get-tuple-element.27), channel_id=1, source_target_pairs={{0,1},{1,2},{2,3},{3,4},{4,5},{5,6},{6,7},{7,8},{8,9},{9,10},{10,1... | collective-permute-start | bytes 24776 | tf_op jit(solution)/shard_map/ppermute | solution.py:16
  33.1 26.4 %slice-start = ((s8[8388608]{0:T(1024)(128)(4,1)}), s8[4194304]{0:T(1024)(128)(4,1)S(1)}, s32[]{:S(2)}) async-start(s8[8388608]{0:T(1024)(128)(4,1)} %bitcast.418), calls=%async_computation.8 | async-start | bytes 8388608
  33.1 5.3 collective-permute-start.3
  39.6 19.9 %slice-start.1 = ((s8[8388608]{0:T(1024)(128)(4,1)}), s8[4194304]{0:T(1024)(128)(4,1)S(1)}, s32[]{:S(2)}) async-start(s8[8388608]{0:T(1024)(128)(4,1)} %bitcast.418), calls=%async_computation.9 | async-start | bytes 8388608
  59.5 13.3 %copy-start.2 = (f32[2048]{0:T(1024)S(1)}, f32[2048]{0:T(1024)}, u32[]{:S(2)}) copy-start(f32[2048]{0:T(1024)} %param.12) | copy-start | bytes 24580
  59.6 13.4 %copy-start.3 = (f32[8]{0:T(128)S(1)}, f32[8]{0:T(128)}, u32[]{:S(2)}) copy-start(f32[8]{0:T(128)} %param.13) | copy-start | bytes 100
  64.0 17.7 %all-to-all-start.1 = ((bf16[32,2,2048]{2,1,0:T(2,128)(2,1)}), bf16[32,2,2048]{2,1,0:T(2,128)(2,1)S(1)}, u32[]{:S(2)}, u32[]{:S(2)}) async-start(bf16[32,2,2048]{2,1,0:T(2,128)(2,1)} %reshape.81), calls=%async_computation.1 | async-start | bytes 524288 | tf_op jit(solution)/shard_map/all_to_all | solution.py:62
  157.0 3.2 collective-permute-start.4
  158.3 5.7 %collective-permute-start.5 = (bf16[8,64,1]{2,0,1:T(8,128)(2,1)S(1)}, bf16[8,64,1]{2,0,1:T(8,128)(2,1)S(1)}, u32[]{:S(2)}, u32[]{:S(2)}) collective-permute-start(bf16[8,64,1]{2,0,1:T(8,128)(2,1)S(1)} %get-tuple-element.38), channel_id=1, source_target_pairs={{32,0},{64,32},{96,64},{128,96},{160,128},{192,160},{224,192},{33,... | collective-permute-start | bytes 3080 | tf_op jit(solution)/shard_map/ppermute | solution.py:17
  164.1 6.9 %collective-permute-start.6 = (bf16[8,1,258]{2,0,1:T(8,128)(2,1)S(1)}, bf16[8,1,258]{2,0,1:T(8,128)(2,1)S(1)}, u32[]{:S(2)}, u32[]{:S(2)}) collective-permute-start(bf16[8,1,258]{2,0,1:T(8,128)(2,1)S(1)} %get-tuple-element.31), channel_id=1, source_target_pairs={{0,1},{1,2},{2,3},{3,4},{4,5},{5,6},{6,7},{7,8},{8,9},{9,10},{10,1... | collective-permute-start | bytes 12392 | tf_op jit(solution)/shard_map/ppermute | solution.py:16
  168.9 4.9 collective-permute-start.7
  440.0 99.5 %copy-start = (f32[8,64,256]{2,1,0:T(8,128)S(1)}, f32[8,64,256]{2,1,0:T(8,128)}, u32[]{:S(2)}) copy-start(f32[8,64,256]{2,1,0:T(8,128)} %param.8) | copy-start | bytes 1572868
  440.2 5.9 %collective-permute-start.8 = (bf16[8,64,1]{2,0,1:T(8,128)(2,1)S(1)}, bf16[8,64,1]{2,0,1:T(8,128)(2,1)S(1)}, u32[]{:S(2)}, u32[]{:S(2)}) collective-permute-start(bf16[8,64,1]{2,0,1:T(8,128)(2,1)S(1)} %get-tuple-element.35), channel_id=1, source_target_pairs={{0,32},{32,64},{64,96},{96,128},{128,160},{160,192},{192,224},{1,3... | collective-permute-start | bytes 3080 | tf_op jit(solution)/shard_map/ppermute | solution.py:16
  443.9 5.7 %collective-permute-start.9 = (bf16[8,64,1]{2,0,1:T(8,128)(2,1)S(1)}, bf16[8,64,1]{2,0,1:T(8,128)(2,1)S(1)}, u32[]{:S(2)}, u32[]{:S(2)}) collective-permute-start(bf16[8,64,1]{2,0,1:T(8,128)(2,1)S(1)} %get-tuple-element.36), channel_id=1, source_target_pairs={{32,0},{64,32},{96,64},{128,96},{160,128},{192,160},{224,192},{33,... | collective-permute-start | bytes 3080 | tf_op jit(solution)/shard_map/ppermute | solution.py:17
  449.7 7.2 %collective-permute-start.10 = (bf16[8,1,258]{2,0,1:T(8,128)(2,1)S(1)}, bf16[8,1,258]{2,0,1:T(8,128)(2,1)S(1)}, u32[]{:S(2)}, u32[]{:S(2)}) collective-permute-start(bf16[8,1,258]{2,0,1:T(8,128)(2,1)S(1)} %get-tuple-element.29), channel_id=1, source_target_pairs={{0,1},{1,2},{2,3},{3,4},{4,5},{5,6},{6,7},{7,8},{8,9},{9,10},{10,1... | collective-permute-start | bytes 12392 | tf_op jit(solution)/shard_map/ppermute | solution.py:16
  453.7 4.9 collective-permute-start.11
